TPU v7x, 128 devices: a whole 4x4x4 slice. The times are simulated.
128 devices in a mesh: row: 16 (over x, y), col: 8 (over z, core).
Axes of the slice: x: 4, y: 4, z: 4, core: 2. Of those that a mesh axis runs over, the one named last changes fastest.
Arguments:
- features: bfloat16 [65536, 256], P(('row', 'col')), may hold values from -6 to 6
- weight: bfloat16 [256, 256], replicated, may hold values from -0.375 to 0.375
- bias: float32 [256], replicated, may hold values from -3 to 3
- adj_blocks: bfloat16 [16, 8, 384, 128, 128], P('row', 'col'), may hold values from -0.21875 to 0.21875
- block_rows: int32 [16, 8, 384], P('row', 'col'), may hold values from 0 to 31
- block_cols: int32 [16, 8, 384], P('row', 'col'), may hold values from 0 to 63
- block_counts: int32 [16, 8], P('row', 'col'), may hold values from 96 to 384, as said below
- grad_out: bfloat16 [65536, 256], P(('row', 'col')), may hold values from -6 to 6
Outputs:
- hidden: bfloat16 [65536, 256], P(('row', 'col'))
- grad_features: bfloat16 [65536, 256], P(('row', 'col'))
- grad_weight: float32 [256, 256], replicated
- grad_bias: float32 [256], replicated
Inputs may be any that keep to these rules, and one draw needn't show every extreme that they name: `block_counts`: number of used entries of each tile's block lists; exactly 384 on some tile of every draw. Entries past it are not part of A. `block_rows`: positions may repeat within a tile. `block_cols`: positions may repeat within a tile.
All inputs are finite; a program needn't handle non-finite values.
Results may differ from a plain program's by a relative error of at most 0.0075.
Values may be sent and summed in bfloat16 or wider, within the bound.
A program may use at most 192 MiB of HBM per device.

v0:
```python
import jax
import jax.numpy as jnp
from jax import lax
from jax.sharding import PartitionSpec as P

GROUP = 128


def silu_grad(value):
    sig = jax.nn.sigmoid(value)
    return sig * (1.0 + value * (1.0 - sig))


def block_product(blocks, outer, inner, count, operand, out_blocks, transposed):
    edge = blocks.shape[-1]
    width = operand.shape[1]
    in_blocks = operand.shape[0] // edge
    flat_tiles = operand.reshape(in_blocks, edge * width)
    form = "bmk,bmf->bkf" if transposed else "bkm,bmf->bkf"
    in_ids = jnp.arange(in_blocks, dtype=jnp.int32)
    out_ids = jnp.arange(out_blocks, dtype=jnp.int32)

    def add_group(step, acc):
        start = step * GROUP
        part = lax.dynamic_slice_in_dim(blocks, start, GROUP, 0)
        rows_in = lax.dynamic_slice_in_dim(inner, start, GROUP, 0)
        rows_out = lax.dynamic_slice_in_dim(outer, start, GROUP, 0)
        selector = (rows_in[:, None] == in_ids[None, :]).astype(operand.dtype)
        taken = jnp.dot(selector, flat_tiles, preferred_element_type=jnp.float32).astype(
            operand.dtype
        )
        taken = taken.reshape(GROUP, edge, width)
        prod = jnp.einsum(form, part, taken, preferred_element_type=jnp.float32)
        live = start + jnp.arange(GROUP, dtype=jnp.int32) < count
        placer = ((out_ids[:, None] == rows_out[None, :]) & live[None, :]).astype(jnp.float32)
        added = jnp.dot(
            placer,
            prod.reshape(GROUP, edge * width),
            preferred_element_type=jnp.float32,
            precision=lax.Precision.HIGHEST,
        )
        return acc + added

    start_acc = jnp.zeros((out_blocks, edge * width), jnp.float32)
    acc = lax.fori_loop(0, blocks.shape[0] // GROUP, add_group, start_acc)
    return acc.reshape(out_blocks * edge, width)


def body(features, weight, bias, adj_blocks, block_rows, block_cols, block_counts, grad_out):
    col_count = lax.axis_size("col")
    row_count = lax.axis_size("row")
    slab = features.shape[0]
    blocks = adj_blocks[0, 0]
    tile_rows = block_rows[0, 0]
    tile_cols = block_cols[0, 0]
    count = block_counts[0, 0]
    edge = blocks.shape[-1]
    panel = jnp.dot(features, weight, preferred_element_type=jnp.float32).astype(jnp.bfloat16)
    panels = lax.all_gather(panel, "row", axis=0, tiled=True)
    partial_value = block_product(
        blocks, tile_rows, tile_cols, count, panels, col_count * slab // edge, False
    )
    pre = lax.psum_scatter(partial_value, "col", scatter_dimension=0, tiled=True)
    active = pre + bias
    hidden = jax.nn.silu(active).astype(jnp.bfloat16)
    own_grad = (grad_out.astype(jnp.float32) * silu_grad(active)).astype(jnp.bfloat16)
    grad_rows = lax.all_gather(own_grad, "col", axis=0, tiled=True)
    bias_term = jnp.sum(own_grad.astype(jnp.float32), axis=0)
    back_partial = block_product(
        blocks, tile_cols, tile_rows, count, grad_rows, row_count * slab // edge, True
    )
    summed = lax.psum(back_partial, "row")
    grad_panel = lax.dynamic_slice_in_dim(summed, lax.axis_index("row") * slab, slab, 0).astype(
        jnp.bfloat16
    )
    grad_features = lax.dot_general(
        grad_panel, weight, (((1,), (1,)), ((), ())), preferred_element_type=jnp.float32
    ).astype(jnp.bfloat16)
    weight_term = lax.dot_general(
        features, grad_panel, (((0,), (0,)), ((), ())), preferred_element_type=jnp.float32
    )
    grad_weight, grad_bias = lax.psum((weight_term, bias_term), ("row", "col"))
    return (hidden, grad_features, grad_weight, grad_bias)


def solution(mesh):
    in_specs = (
        P(("row", "col"), None),
        P(),
        P(),
        P("row", "col", None, None, None),
        P("row", "col", None),
        P("row", "col", None),
        P("row", "col"),
        P(("row", "col"), None),
    )
    out_specs = (P(("row", "col"), None), P(("row", "col"), None), P(), P())
    return jax.shard_map(body, mesh=mesh, in_specs=in_specs, out_specs=out_specs, check_vma=False)
```

profile of v0, /device:TPU:0, one launch (start us, length us, event | category | flops | bytes accessed | tf_op | source)
XLA Modules:
  0.0 912.0 jit_solution(109042561852430651)
XLA Ops:
  7.2 0.9 copy-done
  8.1 1.8 convolution_convert_fusion.3
  10.0 0.7 reduce
  10.7 1.3 reduce.1
  12.0 52.6 %all-gather.3.cloned.1.call-done = bf16[8192,256]{1,0:T(8,128)(2,1)} async-done(((bf16[512,256]{1,0:T(8,128)(2,1)}), bf16[8192,256]{1,0:T(8,128)(2,1)}) %all-gather.3.cloned.1.call-update) | async-done | bytes 4194320 | tf_op jit(solution)/shard_map/all_gather | solution.py:59
  64.6 7.4 reshape.67
  72.0 181.0 %while.28 = (s32[]{:T(128)}, f32[32,32768]{1,0:T(8,128)}, s32[384]{0:T(512)S(1)}, s32[]{:T(128)}, bf16[384,128,128]{2,1,0:T(8,128)(2,1)}, /*index=5*/s32[384]{0:...) while((s32[]{:T(128)}, f32[32,32768]{1,0:T(8,128)}, ...), condition=%wide.region_1.0_spmd.clone, body=%wide.region_0.0_spmd.clone.sunk | while | flops 3227533568 | bytes 117444024 | solution.py:45
  72.0 0.8 dynamic_slice.66
  72.8 7.8 convolution_convert_fusion.6
  80.6 9.1 copy.24
  89.6 12.7 %fusion.53 = f32[128,128,256]{2,1,0:T(8,128)} fusion(bf16[128,128,256]{2,1,0:T(8,128)(2,1)} %bitcast.53, bf16[384,128,128]{2,1,0:T(8,128)(2,1)} %get-tuple-element.524, s32[]{:T(128)S(6)} %select_n.26), kind=kOutput, calls=%fused_computation.6.clone.1 | convolution fusion | flops 1073741824 | bytes 29360132 | tf_op jit(solution)/shard_map/while/body/eval_jaxpr/bkm,bmf->bkf/dot_general | solution.py:33
  102.3 17.7 %copy.25 = f32[16,8,128,256]{3,1,2,0:T(8,128)} copy(f32[16,8,128,256]{3,2,1,0:T(8,128)} %bitcast.51) | data formatting | bytes 33554432 | tf_op jit(solution)/shard_map/while
  120.1 0.7 add_compare_fusion.4
  120.8 11.2 %convolution_add_fusion.4 = f32[32,32768]{1,0:T(8,128)} fusion(f32[128,32768]{1,0:T(8,128)} %bitcast.55, f32[32,32768]{1,0:T(8,128)} %get-tuple-element.510, pred[]{:T(512)S(6)} %compare.6, s32[128]{0:T(128)S(1)} %dynamic_slice.67, pred[128]{0:T(512)(128)(4,1)S(1)} %add_compare_fusion.4), kind=kOutput, calls=%fused_computation.5.clone.1 | convolution fusion | flops 1612718080 | bytes 25166464 | tf_op jit(solution)/shard_map/while/body/eval_jaxpr/dot_general | solution.py:36
  132.0 0.8 dynamic_slice.66
  132.7 7.8 convolution_convert_fusion.6
  140.5 9.1 copy.24
  149.6 12.7 %fusion.53 = f32[128,128,256]{2,1,0:T(8,128)} fusion(bf16[128,128,256]{2,1,0:T(8,128)(2,1)} %bitcast.53, bf16[384,128,128]{2,1,0:T(8,128)(2,1)} %get-tuple-element.524, s32[]{:T(128)S(6)} %select_n.26), kind=kOutput, calls=%fused_computation.6.clone.1 | convolution fusion | flops 1073741824 | bytes 29360132 | tf_op jit(solution)/shard_map/while/body/eval_jaxpr/bkm,bmf->bkf/dot_general | solution.py:33
  162.3 17.7 %copy.25 = f32[16,8,128,256]{3,1,2,0:T(8,128)} copy(f32[16,8,128,256]{3,2,1,0:T(8,128)} %bitcast.51) | data formatting | bytes 33554432 | tf_op jit(solution)/shard_map/while
  180.1 0.7 add_compare_fusion.4
  180.7 11.8 %convolution_add_fusion.4 = f32[32,32768]{1,0:T(8,128)} fusion(f32[128,32768]{1,0:T(8,128)} %bitcast.55, f32[32,32768]{1,0:T(8,128)} %get-tuple-element.510, pred[]{:T(512)S(6)} %compare.6, s32[128]{0:T(128)S(1)} %dynamic_slice.67, pred[128]{0:T(512)(128)(4,1)S(1)} %add_compare_fusion.4), kind=kOutput, calls=%fused_computation.5.clone.1 | convolution fusion | flops 1612718080 | bytes 25166464 | tf_op jit(solution)/shard_map/while/body/eval_jaxpr/dot_general | solution.py:36
  192.5 0.8 dynamic_slice.66
  193.3 7.8 convolution_convert_fusion.6
  201.0 9.1 copy.24
  210.1 12.7 %fusion.53 = f32[128,128,256]{2,1,0:T(8,128)} fusion(bf16[128,128,256]{2,1,0:T(8,128)(2,1)} %bitcast.53, bf16[384,128,128]{2,1,0:T(8,128)(2,1)} %get-tuple-element.524, s32[]{:T(128)S(6)} %select_n.26), kind=kOutput, calls=%fused_computation.6.clone.1 | convolution fusion | flops 1073741824 | bytes 29360132 | tf_op jit(solution)/shard_map/while/body/eval_jaxpr/bkm,bmf->bkf/dot_general | solution.py:33
  222.8 17.7 %copy.25 = f32[16,8,128,256]{3,1,2,0:T(8,128)} copy(f32[16,8,128,256]{3,2,1,0:T(8,128)} %bitcast.51) | data formatting | bytes 33554432 | tf_op jit(solution)/shard_map/while
  240.6 0.7 add_compare_fusion.4
  241.2 11.8 %convolution_add_fusion.4 = f32[32,32768]{1,0:T(8,128)} fusion(f32[128,32768]{1,0:T(8,128)} %bitcast.55, f32[32,32768]{1,0:T(8,128)} %get-tuple-element.510, pred[]{:T(512)S(6)} %compare.6, s32[128]{0:T(128)S(1)} %dynamic_slice.67, pred[128]{0:T(512)(128)(4,1)S(1)} %add_compare_fusion.4), kind=kOutput, calls=%fused_computation.5.clone.1 | convolution fusion | flops 1612718080 | bytes 25166464 | tf_op jit(solution)/shard_map/while/body/eval_jaxpr/dot_general | solution.py:36
  253.0 4.9 reshape.68
  258.0 38.0 %reduce-scatter.2.cloned.1.call-done = f32[512,256]{1,0:T(8,128)} async-done(((f32[4096,256]{1,0:T(8,128)}), f32[512,256]{1,0:T(8,128)}) %reduce-scatter.2.cloned.1.call-update) | async-done | bytes 524304 | tf_op jit(solution)/shard_map/reduce_scatter | solution.py:63
  296.1 2.1 convert_reduce_fusion
  298.2 16.4 %copy.12 = bf16[1,1,384,128,128]{3,4,2,1,0:T(8,128)(2,1)} copy(bf16[1,1,384,128,128]{4,3,2,1,0:T(8,128)(2,1)} %bitcast.60) | data formatting | bytes 25165824 | tf_op args[3]
  314.6 65.2 %psum.23 = f32[256]{0:T(256)} all-reduce(f32[256]{0:T(256)S(1)} %get-tuple-element.409), channel_id=1, replica_groups=mesh['row'=16,'col'=8] {'row','col'}, use_global_device_ids=true, to_apply=%region_8.9 | all-reduce | flops 256 | bytes 2048 | tf_op jit(solution)/shard_map/psum | solution.py:82
  379.7 2.9 reshape.69
  382.6 182.3 %while.29 = (s32[]{:T(128)}, f32[64,32768]{1,0:T(8,128)}, s32[384]{0:T(512)}, s32[]{:T(128)}, bf16[384,128,128]{1,2,0:T(8,128)(2,1)}, /*index=5*/s32[384]{0:T(51...) while((s32[]{:T(128)}, f32[64,32768]{1,0:T(8,128)}, ...), condition=%wide.region_4.5_spmd.clone, body=%wide.region_3.4_spmd.clone.sunk | while | flops 4571811840 | bytes 123735480 | solution.py:45
  382.8 0.1 dynamic_slice.69
  382.9 5.6 convolution_convert_fusion.7
  388.5 9.1 copy.26
  397.6 12.7 %fusion.59 = f32[128,128,256]{2,1,0:T(8,128)} fusion(bf16[128,128,256]{2,1,0:T(8,128)(2,1)} %bitcast.54, bf16[384,128,128]{1,2,0:T(8,128)(2,1)} %get-tuple-element.557, s32[]{:T(128)S(6)} %select_n.27), kind=kOutput, calls=%fused_computation.18.clone.1 | convolution fusion | flops 1073741824 | bytes 29360132 | tf_op jit(solution)/shard_map/while/body/eval_jaxpr/bmk,bmf->bkf/dot_general | solution.py:33
  410.3 17.7 %copy.27 = f32[16,8,128,256]{3,1,2,0:T(8,128)} copy(f32[16,8,128,256]{3,2,1,0:T(8,128)} %bitcast.52) | data formatting | bytes 33554432 | tf_op jit(solution)/shard_map/while
  428.0 0.8 dynamic_slice.70
  428.7 0.7 add_compare_fusion.5
  429.4 13.3 %convolution_add_fusion.5 = f32[64,32768]{1,0:T(8,128)} fusion(f32[128,32768]{1,0:T(8,128)} %bitcast.56, f32[64,32768]{1,0:T(8,128)} %get-tuple-element.543, pred[]{:T(512)S(6)} %compare.7, s32[128]{0:T(128)S(1)} %dynamic_slice.70, pred[128]{0:T(512)(128)(4,1)S(1)} %add_compare_fusion.5), kind=kOutput, calls=%fused_computation.17.clone.1 | convolution fusion | flops 3225436160 | bytes 33555072 | tf_op jit(solution)/shard_map/while/body/eval_jaxpr/dot_general | solution.py:36
  442.7 0.1 dynamic_slice.69
  442.8 5.6 convolution_convert_fusion.7
  448.4 9.1 copy.26
  457.5 12.7 %fusion.59 = f32[128,128,256]{2,1,0:T(8,128)} fusion(bf16[128,128,256]{2,1,0:T(8,128)(2,1)} %bitcast.54, bf16[384,128,128]{1,2,0:T(8,128)(2,1)} %get-tuple-element.557, s32[]{:T(128)S(6)} %select_n.27), kind=kOutput, calls=%fused_computation.18.clone.1 | convolution fusion | flops 1073741824 | bytes 29360132 | tf_op jit(solution)/shard_map/while/body/eval_jaxpr/bmk,bmf->bkf/dot_general | solution.py:33
  470.2 17.7 %copy.27 = f32[16,8,128,256]{3,1,2,0:T(8,128)} copy(f32[16,8,128,256]{3,2,1,0:T(8,128)} %bitcast.52) | data formatting | bytes 33554432 | tf_op jit(solution)/shard_map/while
  487.9 0.8 dynamic_slice.70
  488.7 0.7 add_compare_fusion.5
  489.3 14.5 %convolution_add_fusion.5 = f32[64,32768]{1,0:T(8,128)} fusion(f32[128,32768]{1,0:T(8,128)} %bitcast.56, f32[64,32768]{1,0:T(8,128)} %get-tuple-element.543, pred[]{:T(512)S(6)} %compare.7, s32[128]{0:T(128)S(1)} %dynamic_slice.70, pred[128]{0:T(512)(128)(4,1)S(1)} %add_compare_fusion.5), kind=kOutput, calls=%fused_computation.17.clone.1 | convolution fusion | flops 3225436160 | bytes 33555072 | tf_op jit(solution)/shard_map/while/body/eval_jaxpr/dot_general | solution.py:36
  503.9 5.6 convolution_convert_fusion.7
  509.5 9.1 copy.26
  518.6 12.7 %fusion.59 = f32[128,128,256]{2,1,0:T(8,128)} fusion(bf16[128,128,256]{2,1,0:T(8,128)(2,1)} %bitcast.54, bf16[384,128,128]{1,2,0:T(8,128)(2,1)} %get-tuple-element.557, s32[]{:T(128)S(6)} %select_n.27), kind=kOutput, calls=%fused_computation.18.clone.1 | convolution fusion | flops 1073741824 | bytes 29360132 | tf_op jit(solution)/shard_map/while/body/eval_jaxpr/bmk,bmf->bkf/dot_general | solution.py:33
  531.3 17.7 %copy.27 = f32[16,8,128,256]{3,1,2,0:T(8,128)} copy(f32[16,8,128,256]{3,2,1,0:T(8,128)} %bitcast.52) | data formatting | bytes 33554432 | tf_op jit(solution)/shard_map/while
  549.0 0.8 dynamic_slice.70
  549.8 0.7 add_compare_fusion.5
  550.4 14.5 %convolution_add_fusion.5 = f32[64,32768]{1,0:T(8,128)} fusion(f32[128,32768]{1,0:T(8,128)} %bitcast.56, f32[64,32768]{1,0:T(8,128)} %get-tuple-element.543, pred[]{:T(512)S(6)} %compare.7, s32[128]{0:T(128)S(1)} %dynamic_slice.70, pred[128]{0:T(512)(128)(4,1)S(1)} %add_compare_fusion.5), kind=kOutput, calls=%fused_computation.17.clone.1 | convolution fusion | flops 3225436160 | bytes 33555072 | tf_op jit(solution)/shard_map/while/body/eval_jaxpr/dot_general | solution.py:36
  565.0 9.3 %reshape.70 = f32[8192,256]{1,0:T(8,128)} reshape(f32[64,32768]{1,0:T(8,128)} %get-tuple-element.313) | data formatting | bytes 16777216 | tf_op jit(solution)/shard_map/reshape | solution.py:46
  574.2 189.9 %all-reduce.4 = bf16[8192,256]{1,0:T(8,128)(2,1)} all-reduce(f32[8192,256]{1,0:T(8,128)} %reshape.70), channel_id=1, replica_groups=mesh['row'=16,'col'=8] {'row'}, use_global_device_ids=true, to_apply=%region_5.6 | all-reduce | flops 2097152 | bytes 12582912 | tf_op jit(solution)/shard_map/psum | solution.py:72
  764.1 1.9 convolution_bitcast_fusion
  766.0 1.9 convolution_convert_fusion.2
  768.0 135.7 %all-reduce.3.cloned.1.call-done = f32[256,256]{0,1:T(8,128)} async-done(((f32[256,256]{0,1:T(8,128)}), f32[256,256]{0,1:T(8,128)}) %all-reduce.3.cloned.1.call-update) | async-done | bytes 262160 | tf_op jit(solution)/shard_map/psum | solution.py:82
  903.7 1.8 copy.14
  (22 shorter events, 0.5 us)
Async XLA Ops:
  7.2 1.0 copy-start
  7.2 57.4 %all-gather.3.cloned.1.call-start = ((), (), s32[]{:S(2)}) async-start(), calls=%async_computation.1 | async-start | bytes 4456448 | tf_op jit(solution)/shard_map/all_gather | solution.py:59
  10.0 286.1 %reduce-scatter.2.cloned.1.call-start = ((), (), s32[]{:S(2)}) async-start(), calls=%async_computation.2 | async-start | bytes 4718592 | tf_op jit(solution)/shard_map/reduce_scatter | solution.py:63
  253.0 43.0 %copy-start.2 = (bf16[512,256]{1,0:T(8,128)(2,1)S(1)}, bf16[512,256]{1,0:T(8,128)(2,1)}, u32[]{:S(2)}) copy-start(bf16[512,256]{1,0:T(8,128)(2,1)} %param.19) | copy-start | bytes 786436
  253.0 43.0 %copy-start.3 = (f32[256]{0:T(256)S(1)}, f32[256]{0:T(256)}, u32[]{:S(2)}) copy-start(f32[256]{0:T(256)} %param.14) | copy-start | bytes 3076
  258.0 121.8 %all-gather.5.cloned.1.call-start = ((), (), s32[]{:S(2)}) async-start(), calls=%async_computation.3 | async-start | bytes 2359296 | tf_op jit(solution)/shard_map/all_gather | solution.py:67
  298.2 605.5 %all-reduce.3.cloned.1.call-start = ((), (), s32[]{:S(2)}) async-start(), calls=%async_computation.4 | async-start | bytes 524288 | tf_op jit(solution)/shard_map/psum | solution.py:82
  574.2 191.8 %copy-start.1 = (bf16[256,256]{1,0:T(8,128)(2,1)S(1)}, bf16[256,256]{1,0:T(8,128)(2,1)}, u32[]{:S(2)}) copy-start(bf16[256,256]{1,0:T(8,128)(2,1)} %param.13) | copy-start | bytes 393220
Sparse Core Ops, SparseCore 0:
  10.7 53.8 all-gather.2
  258.1 37.9 reduce-scatter.1
  298.3 24.0 all-gather.4
  766.2 137.4 all-reduce.2
where the time goes:
time: 915 us; the launch traced here: 912 us
  blocking collectives  255 us (28%)
  waiting for transfers between devices  226 us (25%)
  local copies, waits for them, and re-layouts  209 us (23%)
  matrix products  199 us (22%)
  between operations  13.8 us (2%)
    psum x1, blocking collectives, body(): summed = lax.psum(back_partial, 'row')  190 us
    while x12, local copies, waits for them, and re-layouts  161 us
    psum x1, waiting for transfers between devices, body(): grad_weight, grad_bias = lax.psum((weight_term, bias_term), ('row', 'col'))  136 us
    dot_general x6, matrix products, add_group(): jnp.dot(placer, prod.reshape(GROUP, edge * width), preferred_element_type...  77.2 us
    dot_general x6, matrix products, add_group(): prod = jnp.einsum(form, part, taken, preferred_element_type=jnp.float32)  76.2 us
    psum x1, blocking collectives, body(): grad_weight, grad_bias = lax.psum((weight_term, bias_term), ('row', 'col'))  65.2 us
    all_gather x1, waiting for transfers between devices, body(): panels = lax.all_gather(panel, 'row', axis=0, tiled=True)  52.6 us
    dot_general x6, matrix products, add_group(): jnp.dot(selector, flat_tiles, preferred_element_type=jnp.float32)  40.1 us
  transfers between devices with their start and end apart: 4, of which 3 were waited for; matrix products, arithmetic and copies ran while one was open for 2% of the time, Pallas kernels for 0%

commit v1 on v0

v1 whole, which is shorter than its diff:
```python
import functools

import jax
import jax.numpy as jnp
from jax import lax
from jax.experimental import pallas as pl
from jax.experimental.pallas import tpu as pltpu
from jax.sharding import PartitionSpec as P

MESH = pl.DeviceIdType.MESH
VMEM = pltpu.VMEM
SMEM = pltpu.SMEM
BF16 = jnp.bfloat16
F32 = jnp.float32
I32 = jnp.int32
EDGE = 128
WIDE = 128
HALVES = 2
SLOTS = 512
MAXB = 384
ROW_BLOCKS = 32
COL_BLOCKS = 64
FWD_STEPS = (MAXB + ROW_BLOCKS) // 2
BWD_STEPS = (MAXB + COL_BLOCKS) // 2
UNROLL = 16
PART = 40


def dot(a, b):
    return jnp.dot(a, b, preferred_element_type=F32)


def dot_nt(a, b):
    return lax.dot_general(a, b, (((1,), (1,)), ((), ())), preferred_element_type=F32)


def dot_tn(a, b):
    return lax.dot_general(a, b, (((0,), (0,)), ((), ())), preferred_element_type=F32)


def one_table(outer, inner, count, table):
    ids = lax.broadcasted_iota(I32, (1, MAXB), 1)
    key = jnp.where(ids < count, outer, -1)
    lanes = lax.broadcasted_iota(I32, (EDGE, MAXB), 0)
    member = (lanes == key).astype(F32)
    member16 = member.astype(BF16)
    before = (
        lax.broadcasted_iota(I32, (MAXB, MAXB), 0) < lax.broadcasted_iota(I32, (MAXB, MAXB), 1)
    ).astype(F32).astype(BF16)
    within = jnp.sum(member * dot(member16, before), axis=0, keepdims=True)
    held = jnp.sum(member, axis=1, keepdims=True).astype(I32)
    pairs = ((held + 1) >> 1).astype(F32)
    start = jnp.sum((lanes < key).astype(F32) * pairs, axis=0, keepdims=True)
    place = jnp.where(key >= 0, (2.0 * start + within).astype(I32), -1)
    taken = (lax.broadcasted_iota(I32, (SLOTS, MAXB), 0) == place).astype(F32).astype(BF16)
    which = lax.broadcasted_iota(I32, (8, MAXB), 0)
    low = jnp.broadcast_to(ids & 127, (8, MAXB))
    high = jnp.broadcast_to(ids >> 7, (8, MAXB))
    operand = jnp.broadcast_to(inner, (8, MAXB))
    first = jnp.broadcast_to((within < 0.5).astype(I32), (8, MAXB))
    values = jnp.where(which == 0, low, jnp.where(which == 1, high, jnp.where(which == 2, operand, jnp.where(which == 3, first, 1))))
    picked = dot_nt(values.astype(F32).astype(BF16), taken).astype(I32)
    table[0:1, :] = jnp.where(picked[4:5, :] > 0, picked[0:1, :] + EDGE * picked[1:2, :], MAXB)
    table[1:2, :] = picked[2:3, :]
    table[2:3, :] = 1 - picked[3:4, :]
    held_row = dot_nt(jnp.ones((8, MAXB), BF16), member16).astype(I32)
    pairs_row = ((held_row + 1) >> 1).astype(F32).astype(BF16)
    upto = (
        lax.broadcasted_iota(I32, (EDGE, EDGE), 0) <= lax.broadcasted_iota(I32, (EDGE, EDGE), 1)
    ).astype(F32).astype(BF16)
    ends = jnp.maximum(dot(pairs_row, upto).astype(I32) - 1, 0)
    table[3:4, 0:EDGE] = ends[0:1, :]
    table[4:5, 0:EDGE] = (held_row[0:1, :] > 0).astype(I32)


def table_kernel(count, rows, cols, fwd, bwd):
    fwd[...] = jnp.zeros_like(fwd)
    bwd[...] = jnp.zeros_like(bwd)
    one_table(rows[0], cols[0], count[0, 0], fwd)
    one_table(cols[0], rows[0], count[0, 0], bwd)


def make_tables(block_rows, block_cols, block_counts):
    shape = jax.ShapeDtypeStruct((8, SLOTS), I32)
    return pl.pallas_call(
        table_kernel,
        out_shape=(shape, shape),
        in_specs=[pl.BlockSpec(memory_space=SMEM)] + [pl.BlockSpec(memory_space=VMEM)] * 2,
        out_specs=(pl.BlockSpec(memory_space=VMEM),) * 2,
    )(block_counts, block_rows, block_cols)


def layer_kernel(
    fwd, bwd, feat, weight, bias, blocks_hbm, gout,
    hidden, gfeat, gweight, gbias,
    blocks, x0, x1, segs, sib_out, sib_in, z_out, z_in, ax, gp, gt0, gt1,
    a_out, a_in, b_out, b_in, a2_out, a2_in, b2_out, b2_in,
    ar_mine, ar_cols, ar_x, ar_y, ar_all,
    blocks_sem, x_send, x_recv, sib_send, sib_recv, z_send, z_recv, g_send, g_recv,
    c_send, c_recv, r_send, r_recv, ar_send, ar_recv,
):
    row = lax.axis_index("row")
    col = lax.axis_index("col")
    x, y = row // 4, row % 4
    z, core = col // 2, col % 2
    xs = (x0, x1)
    gts = (gt0, gt1)

    def at_x(d):
        return (lax.rem(x + d + 4, 4) * 4 + y, col)

    def at_y(d):
        return (x * 4 + lax.rem(y + d + 4, 4), col)

    def at_z(d):
        return (row, lax.rem(z + d + 4, 4) * 2 + core)

    sibling = (row, z * 2 + 1 - core)

    def remote(src, dst, send, recv, to):
        return pltpu.make_async_remote_copy(
            src_ref=src, dst_ref=dst, send_sem=send, recv_sem=recv, device_id=to, device_id_type=MESH
        )

    load = pltpu.make_async_copy(blocks_hbm.at[0, 0], blocks.at[pl.ds(0, MAXB)], blocks_sem)
    load.start()
    barrier = pltpu.get_barrier_semaphore()
    for d in range(1, 4):
        for to in (at_x(d), at_y(d)):
            pl.semaphore_signal(barrier, inc=1, device_id=to, device_id_type=MESH)
    for d in range(1, 8):
        to = (row, lax.rem(col + d, 8))
        pl.semaphore_signal(barrier, inc=1, device_id=to, device_id_type=MESH)

    for h in range(HALVES):
        xs[h][x, y] = feat[:, h * WIDE:(h + 1) * WIDE].reshape(4, EDGE, WIDE)
    blocks[MAXB] = jnp.zeros((EDGE, EDGE), BF16)
    pl.semaphore_wait(barrier, 13)

    def slab(h, half, e, d):
        first = lax.rem((x if half == 0 else y) - e + 4, 4)
        second = lax.rem((y if half == 0 else x) - d + 4, 4)
        return (first, second) if half == 0 else (second, first)

    def x_copy(h, half, e, d, q, n, sem, to):
        i, j = slab(h, half, e, d)
        part = xs[h].at[i, j, pl.ds(q, n)]
        return remote(part, part, x_send.at[h, half, sem], x_recv.at[h, half, sem], to)

    firsts = (at_x, at_y)
    seconds = (at_y, at_x)

    def x_along(h, half, d):
        return x_copy(h, half, 0, 0, 2 * half, 2, d - 1, firsts[half](d))

    def x_across(h, half, e, way):
        return x_copy(h, half, e, 0, 2 * half, 2, 3 + e * 4 + way, seconds[half](1 - 2 * way))

    def x_pass(h, half, e, way):
        return x_copy(
            h, half, e, 1 - 2 * way, 2 * half + way, 1, 5 + e * 4 + way, seconds[half](1 - 2 * way)
        )

    def x_start(h):
        for half in range(2):
            for d in (1, 3, 2):
                x_along(h, half, d).start()
            for way in range(2):
                x_across(h, half, 0, way).start()

    def x_step(h, e):
        for half in range(2):
            x_along(h, half, e).wait_recv()
            for way in range(2):
                x_across(h, half, e, way).start()

    def x_forward(h, e):
        for half in range(2):
            for way in range(2):
                x_across(h, half, e, way).wait_recv()
                x_pass(h, half, e, way).start()

    def x_finish(h):
        for e in range(4):
            for half in range(2):
                for way in range(2):
                    x_pass(h, half, e, way).wait_recv()

    def x_drain(h):
        for half in range(2):
            for d in (1, 2, 3):
                x_along(h, half, d).wait_send()
            for e in range(4):
                for way in range(2):
                    x_across(h, half, e, way).wait_send()
                    x_pass(h, half, e, way).wait_send()

    def products(table, steps, one, between):
        trips = steps // UNROLL
        cuts = [trips * i // len(between) for i in range(len(between) + 1)]

        def trip(i, acc):
            for u in range(UNROLL):
                k = i * UNROLL + u
                keep = table[2, 2 * k].astype(F32)
                acc = acc * keep + one(table[0, 2 * k], table[0, 2 * k + 1], table[1, 2 * k], table[1, 2 * k + 1])
                segs[k] = acc.astype(BF16)
            return acc

        acc = jnp.zeros((EDGE, WIDE), F32)
        for i, act in enumerate(between):
            act()
            acc = lax.fori_loop(cuts[i], cuts[i + 1], trip, acc)

    def forward(h, between):
        def one(b0, b1, c0, c1):
            i0, j0, q0 = c0 // 16, (c0 // 4) % 4, c0 % 4
            i1, j1, q1 = c1 // 16, (c1 // 4) % 4, c1 % 4
            pair = jnp.concatenate([blocks[b0], blocks[b1]], axis=1)
            taken = jnp.concatenate([xs[h][i0, j0, q0], xs[h][i1, j1, q1]], axis=0)
            return dot(pair, taken)

        products(fwd, FWD_STEPS, one, between)

    def backward(h, between):
        def one(b0, b1, r0, r1):
            pair = jnp.concatenate([blocks[b0], blocks[b1]], axis=0)
            taken = jnp.concatenate(
                [gts[h][r0 // 4, r0 % 4], gts[h][r1 // 4, r1 % 4]], axis=1
            )
            return dot(taken, pair)

        products(bwd, BWD_STEPS, one, between)

    def segment(table, r):
        return segs[table[3, r]] * table[4, r].astype(F32).astype(BF16)

    def sib_copy(h, d):
        return remote(sib_out.at[h, d], sib_in.at[h, d], sib_send.at[h, d], sib_recv.at[h, d], sibling)

    def z_copy(h, d):
        return remote(z_out.at[h, d], z_in.at[h, d], z_send.at[h, d], z_recv.at[h, d], at_z(d))

    def sum_start(h):
        for d in (1, 3, 2, 0):
            zz = lax.rem(z + d, 4)
            for q in range(4):
                sib_out[h, d, q] = segment(fwd, (zz * 2 + 1 - core) * 4 + q)
            sib_copy(h, d).start()
        for d in (1, 3, 2, 0):
            zz = lax.rem(z + d, 4)
            for q in range(4):
                z_out[h, d, q] = segment(fwd, (zz * 2 + core) * 4 + q)

    def sum_step(h):
        for d in (1, 3, 2):
            sib_copy(h, d).wait_recv()
            for q in range(4):
                z_out[h, d, q] = (z_out[h, d, q].astype(F32) + sib_in[h, d, q].astype(F32)).astype(BF16)
            z_copy(h, d).start()
        sib_copy(h, 0).wait_recv()

    def sum_finish(h):
        for d in (1, 3, 2):
            z_copy(h, d).wait_recv()
        for q in range(4):
            total = z_out[h, 0, q].astype(F32) + sib_in[h, 0, q].astype(F32)
            for d in (1, 3, 2):
                total = total + z_in[h, d, q].astype(F32)
            ax[q * EDGE:(q + 1) * EDGE, h * WIDE:(h + 1) * WIDE] = total

    def g_part(h, d, k):
        return gts[h].at[lax.rem(z + d + 4, 4) * 2 + k]

    def g_across(h, d):
        part = g_part(h, 0, core)
        return remote(part, part, g_send.at[h, d - 1], g_recv.at[h, d - 1], at_z(d))

    def g_sibling(h, d):
        part = g_part(h, -d, core)
        return remote(part, part, g_send.at[h, 3 + d], g_recv.at[h, 3 + d], sibling)

    def g_start(h):
        for d in (1, 3, 2):
            g_across(h, d).start()
        g_sibling(h, 0).start()

    def g_step(h):
        for d in (1, 3, 2):
            g_across(h, d).wait_recv()
            g_sibling(h, d).start()
        for d in (0, 1, 3, 2):
            g_sibling(h, d).wait_recv()

    outs, ins = (a_out, b_out), (a_in, b_in)
    outs2, ins2 = (a2_out, b2_out), (a2_in, b2_in)

    def c_copy(h, half, d):
        return remote(
            outs[half].at[h, d], ins[half].at[h, d], c_send.at[h, half, d], c_recv.at[h, half, d], firsts[half](d)
        )

    def r_copy(h, half, d):
        return remote(
            outs2[half].at[h, d], ins2[half].at[h, d], r_send.at[h, half, d], r_recv.at[h, half, d], seconds[half](d)
        )

    def back_gather(h, d):
        for half in range(2):
            for s in range(4):
                first = lax.rem((x if half == 0 else y) + d, 4)
                second = lax.rem((y if half == 0 else x) + s, 4)
                i, j = (first, second) if half == 0 else (second, first)
                for q in range(2):
                    outs[half][h, d, s, q] = segment(bwd, (i * 4 + j) * 4 + 2 * half + q)

    def back_start(h):
        for d in (1, 3, 2):
            back_gather(h, d)
            for half in range(2):
                c_copy(h, half, d).start()
        back_gather(h, 0)

    def back_step(h):
        for half in range(2):
            for d in (1, 3, 2):
                c_copy(h, half, d).wait_recv()
        for s in (1, 3, 2, 0):
            for half in range(2):
                for q in range(2):
                    total = outs[half][h, 0, s, q].astype(F32)
                    for d in (1, 3, 2):
                        total = total + ins[half][h, d, s, q].astype(F32)
                    outs2[half][h, s, q] = total.astype(BF16)
                if s:
                    r_copy(h, half, s).start()

    def back_finish(h):
        for half in range(2):
            for d in (1, 3, 2):
                r_copy(h, half, d).wait_recv()
            for q in range(2):
                total = outs2[half][h, 0, q].astype(F32)
                for d in (1, 3, 2):
                    total = total + ins2[half][h, d, q].astype(F32)
                b = 2 * half + q
                gfeat[b * EDGE:(b + 1) * EDGE, h * WIDE:(h + 1) * WIDE] = jnp.transpose(total).astype(BF16)

    def ar_scatter(d):
        to = lax.rem(col + d, 8)
        return remote(ar_mine.at[to], ar_cols.at[col], ar_send.at[d], ar_recv.at[d], (row, to))

    def ar_over_x(d):
        return remote(ar_x.at[x], ar_x.at[x], ar_send.at[7 + d], ar_recv.at[7 + d], at_x(d))

    def ar_over_y(d):
        return remote(ar_y.at[y], ar_y.at[y], ar_send.at[10 + d], ar_recv.at[10 + d], at_y(d))

    def ar_gather(d):
        to = lax.rem(col + d, 8)
        return remote(ar_all.at[col], ar_all.at[col], ar_send.at[13 + d], ar_recv.at[13 + d], (row, to))

    def ar_start():
        for d in range(1, 8):
            ar_scatter(d).start()
        ar_cols[col] = ar_mine[col]

    def ar_step1():
        for d in range(1, 8):
            ar_scatter(d).wait_recv()
        total = ar_cols[0]
        for i in range(1, 8):
            total = total + ar_cols[i]
        ar_x[x] = total
        for d in range(1, 4):
            ar_over_x(d).start()

    def ar_step2():
        for d in range(1, 4):
            ar_over_x(d).wait_recv()
        ar_y[y] = (ar_x[0] + ar_x[1]) + (ar_x[2] + ar_x[3])
        for d in range(1, 4):
            ar_over_y(d).start()

    def ar_step3():
        for d in range(1, 4):
            ar_over_y(d).wait_recv()
        ar_all[col] = (ar_y[0] + ar_y[1]) + (ar_y[2] + ar_y[3])
        for d in range(1, 8):
            ar_gather(d).start()

    def ar_finish():
        for d in range(1, 8):
            ar_gather(d).wait_recv()
        for i in range(8):
            gweight[i * 32:(i + 1) * 32, :] = ar_all[i, 0:32, :]
        gbias[...] = ar_all[0, 32:33, :]

    def nothing():
        pass

    x_start(0)
    for e in (1, 3, 2):
        x_step(0, e)
    x_start(1)
    for e in (0, 1, 3, 2):
        x_forward(0, e)
    for e in (1, 3, 2):
        x_step(1, e)
    x_finish(0)
    load.wait()
    forward(0, [functools.partial(x_forward, 1, e) for e in (0, 1, 3, 2)] + [nothing])
    sum_start(0)
    sum_step(0)
    x_finish(1)
    forward(1, [nothing])
    sum_start(1)
    sum_finish(0)
    sum_step(1)
    sum_finish(1)

    bias_sum = jnp.zeros((1, HALVES * WIDE), F32)
    for q in range(4):
        at = slice(q * EDGE, (q + 1) * EDGE)
        total = ax[at, :]
        high = total.astype(BF16)
        low = (total - high.astype(F32)).astype(BF16)
        value = dot(high, weight[...]) + dot(low, weight[...]) + bias[...]
        sig = 1.0 / (1.0 + jnp.exp(-value))
        grad = (gout[at, :].astype(F32) * (sig * (1.0 + value * (1.0 - sig)))).astype(BF16)
        hidden[at, :] = (value * sig).astype(BF16)
        gp[at, :] = grad
        bias_sum = bias_sum + jnp.sum(grad.astype(F32), axis=0, keepdims=True)
        turned = dot_nt(weight[...], grad).astype(BF16)
        for h in range(HALVES):
            gts[h][col, q] = turned[h * WIDE:(h + 1) * WIDE, :]
    g_start(0)
    g_start(1)
    total = ax[...]
    high = total.astype(BF16)
    low = (total - high.astype(F32)).astype(BF16)
    weight_term = dot_tn(high, gp[...]) + dot_tn(low, gp[...])
    for i in range(8):
        ar_mine[i, 0:32, :] = weight_term[i * 32:(i + 1) * 32, :]
        ar_mine[i, 32:PART, :] = jnp.broadcast_to(bias_sum, (PART - 32, HALVES * WIDE))
    g_step(0)
    ar_start()
    backward(0, [nothing])
    back_start(0)
    ar_step1()
    g_step(1)
    backward(1, [nothing, ar_step2, ar_step3])
    back_start(1)
    back_step(0)
    ar_finish()
    back_finish(0)
    back_step(1)
    back_finish(1)

    for h in range(HALVES):
        x_drain(h)
        for d in range(4):
            sib_copy(h, d).wait_send()
            g_sibling(h, d).wait_send()
        for d in range(1, 4):
            z_copy(h, d).wait_send()
            g_across(h, d).wait_send()
            for half in range(2):
                c_copy(h, half, d).wait_send()
                r_copy(h, half, d).wait_send()
    for d in range(1, 4):
        ar_over_x(d).wait_send()
        ar_over_y(d).wait_send()
    for d in range(1, 8):
        ar_scatter(d).wait_send()
        ar_gather(d).wait_send()


def body(features, weight, bias, adj_blocks, block_rows, block_cols, block_counts, grad_out):
    nodes, hid = features.shape
    fwd, bwd = make_tables(block_rows, block_cols, block_counts)
    sem = pltpu.SemaphoreType.DMA
    block = (EDGE, EDGE)
    vmem = pl.BlockSpec(memory_space=VMEM)
    smem = pl.BlockSpec(memory_space=SMEM)
    hidden, grad_features, grad_weight, grad_bias = pl.pallas_call(
        layer_kernel,
        out_shape=(
            jax.ShapeDtypeStruct((nodes, hid), BF16),
            jax.ShapeDtypeStruct((nodes, hid), BF16),
            jax.ShapeDtypeStruct((hid, hid), F32),
            jax.ShapeDtypeStruct((1, hid), F32),
        ),
        in_specs=[smem, smem, vmem, vmem, vmem, pl.BlockSpec(memory_space=pl.ANY), vmem],
        out_specs=(vmem,) * 4,
        scratch_shapes=[
            VMEM((MAXB + 8, EDGE, EDGE), BF16),
            VMEM((4, 4, 4) + block, BF16),
            VMEM((4, 4, 4) + block, BF16),
            VMEM((BWD_STEPS,) + block, BF16),
            VMEM((HALVES, 4, 4) + block, BF16),
            VMEM((HALVES, 4, 4) + block, BF16),
            VMEM((HALVES, 4, 4) + block, BF16),
            VMEM((HALVES, 4, 4) + block, BF16),
            VMEM((nodes, hid), F32),
            VMEM((nodes, hid), BF16),
            VMEM((8, 4) + block, BF16),
            VMEM((8, 4) + block, BF16),
            VMEM((HALVES, 4, 4, 2) + block, BF16),
            VMEM((HALVES, 4, 4, 2) + block, BF16),
            VMEM((HALVES, 4, 4, 2) + block, BF16),
            VMEM((HALVES, 4, 4, 2) + block, BF16),
            VMEM((HALVES, 4, 2) + block, BF16),
            VMEM((HALVES, 4, 2) + block, BF16),
            VMEM((HALVES, 4, 2) + block, BF16),
            VMEM((HALVES, 4, 2) + block, BF16),
            VMEM((8, PART, hid), F32),
            VMEM((8, PART, hid), F32),
            VMEM((4, PART, hid), F32),
            VMEM((4, PART, hid), F32),
            VMEM((8, PART, hid), F32),
            sem,
            sem((HALVES, 2, 19)), sem((HALVES, 2, 19)),
            sem((HALVES, 4)), sem((HALVES, 4)),
            sem((HALVES, 4)), sem((HALVES, 4)),
            sem((HALVES, 7)), sem((HALVES, 7)),
            sem((HALVES, 2, 4)), sem((HALVES, 2, 4)),
            sem((HALVES, 2, 4)), sem((HALVES, 2, 4)),
            sem((21,)), sem((21,)),
        ],
        compiler_params=pltpu.CompilerParams(
            collective_id=0, has_side_effects=True, vmem_limit_bytes=56 * 2**20
        ),
        cost_estimate=pl.CostEstimate(flops=8 * 10**9, bytes_accessed=16 * 2**20, transcendentals=2**18),
    )(fwd, bwd, features, weight, bias.reshape(1, hid), adj_blocks, grad_out)
    return hidden, grad_features, grad_weight, grad_bias.reshape(hid)


def solution(mesh):
    in_specs = (
        P(("row", "col"), None),
        P(),
        P(),
        P("row", "col", None, None, None),
        P("row", "col", None),
        P("row", "col", None),
        P("row", "col"),
        P(("row", "col"), None),
    )
    out_specs = (P(("row", "col"), None), P(("row", "col"), None), P(), P())
    return jax.shard_map(body, mesh=mesh, in_specs=in_specs, out_specs=out_specs, check_vma=False)
```

time: 915 us -> 133 us (0.15)
  blocking collectives: 255 us -> 0 us
  waiting for transfers between devices: 226 us -> 0 us
  local copies, waits for them, and re-layouts: 209 us -> 6.22 us
  matrix products: 199 us -> 0 us
  Pallas kernels: 0 us -> 125 us
  between operations: 13.8 us -> 1.29 us
    psum x2 -> x0, blocking collectives: 255 us -> none  [the longest x1 190 us: body(): summed = lax.psum(back_partial, 'row')]
    dot_general x21 -> x0, matrix products: 199 us -> none  [the longest x6 77.2 us: add_group(): jnp.dot(placer, prod.reshape(GROUP, edge * width), preferred_element_type...]
    while x12 -> x0, local copies, waits for them, and re-layouts: 161 us -> none
    psum x1 -> x0, waiting for transfers between devices: 136 us -> none  [body(): grad_weight, grad_bias = lax.psum((weight_term, bias_term), ('row', 'col'))]
    pallas_call x0 -> x2, Pallas kernels: none -> 125 us  [the longest x1 123 us: body(): pl.pallas_call(layer_kernel, out_shape=(jax.ShapeDtypeStruct((nodes, hid)...]
    all_gather x2 -> x0, waiting for transfers between devices: 52.6 us -> none  [the longest x1 52.6 us: body(): panels = lax.all_gather(panel, 'row', axis=0, tiled=True)]
    reduce_scatter x1 -> x0, waiting for transfers between devices: 38 us -> none  [body(): lax.psum_scatter(partial_value, 'col', scatter_dimension=0, tiled=True)]
    reshape x4 -> x0, local copies, waits for them, and re-layouts: 24.5 us -> none  [the longest x2 14.2 us: block_product(): return acc.reshape(out_blocks * edge, width)]
  transfers between devices with their start and end apart: 4 -> 0, of which waited for: 3 -> 0; matrix products, arithmetic and copies ran while one was open for 2% -> 0% of each run, Pallas kernels for 0% -> 0%
where the time goes in v1:
time: 133 us
  Pallas kernels  125 us (94%)
  local copies, waits for them, and re-layouts  6.22 us (5%)
    pallas_call x1, Pallas kernels, body(): pl.pallas_call(layer_kernel, out_shape=(jax.ShapeDtypeStruct((nodes, hid)...  123 us
    unnamed x4, local copies, waits for them, and re-layouts  6.22 us

profile of v1, /device:TPU:0, one launch (start us, length us, event | category | flops | bytes accessed | tf_op | source)
XLA Modules:
  0.0 132.8 jit_solution(7540515548047829218)
XLA Ops:
  1.3 2.4 %shard_map.111 = (s32[8,512]{1,0:T(8,128)}, s32[8,512]{1,0:T(8,128)}) custom-call(s32[1,1]{1,0:T(1,128)S(6)} %copy.16.count, s32[1,1,384]{2,1,0:T(1,128)} %rows.1, s32[1,1,384]{2,1,0:T(1,128)} %cols.1), custom_call_target="tpu_custom_call" | custom-call | tf_op jit(solution)/shard_map/pallas_call | solution.py:85
  3.7 122.8 %shard_map.112 = (bf16[512,256]{1,0:T(8,128)(2,1)}, bf16[512,256]{1,0:T(8,128)(2,1)}, f32[256,256]{1,0:T(8,128)}, f32[1,256]{1,0:T(1,128)}) custom-call(s32[8,512]{1,0:T(8,128)} %get-tuple-element.10.fwd, s32[8,512]{1,0:T(8,128)} %get-tuple-element.11.bwd, bf16[512,256]{1,0:T(8,128)(2,1)} %feat.1, bf16[256,256]{1,0:T(8,128)(2,1)} %weight.1, ...), custom_call_target="tpu_custom_call" | custom-call | flops 8000000000 | bytes 16777216 | tf_op jit(solution)/shard_map/pallas_call | solution.py:486
  126.5 1.7 %copy.17 = bf16[512,256]{1,0:T(8,128)(2,1)} copy(bf16[512,256]{1,0:T(8,128)(2,1)} %get-tuple-element.20) | data formatting | bytes 524288
  128.2 1.7 %copy.18 = bf16[512,256]{1,0:T(8,128)(2,1)} copy(bf16[512,256]{1,0:T(8,128)(2,1)} %get-tuple-element.21) | data formatting | bytes 524288
  129.9 1.7 %copy.19 = f32[256,256]{1,0:T(8,128)} copy(f32[256,256]{1,0:T(8,128)} %get-tuple-element.22) | data formatting | bytes 524288
  131.5 1.2 copy.20

commit v2 on v1

v2 whole, which is shorter than its diff:
```python
import functools

import jax
import jax.numpy as jnp
from jax import lax
from jax.experimental import pallas as pl
from jax.experimental.pallas import tpu as pltpu
from jax.sharding import PartitionSpec as P

MESH = pl.DeviceIdType.MESH
VMEM = pltpu.VMEM
SMEM = pltpu.SMEM
BF16 = jnp.bfloat16
F32 = jnp.float32
I32 = jnp.int32
EDGE = 128
WIDE = 128
HALVES = 2
THIN = 64
CHUNKS = 4
SLOTS = 512
MAXB = 384
ROW_BLOCKS = 32
COL_BLOCKS = 64
FWD_STEPS = (MAXB + ROW_BLOCKS) // 2
BWD_STEPS = (MAXB + COL_BLOCKS) // 2
FWD_UNROLL = 26
BWD_UNROLL = 32
PART = 40


def dot(a, b):
    return jnp.dot(a, b, preferred_element_type=F32)


def dot_nt(a, b):
    return lax.dot_general(a, b, (((1,), (1,)), ((), ())), preferred_element_type=F32)


def dot_tn(a, b):
    return lax.dot_general(a, b, (((0,), (0,)), ((), ())), preferred_element_type=F32)


def one_table(outer, inner, count, table):
    ids = lax.broadcasted_iota(I32, (1, MAXB), 1)
    key = jnp.where(ids < count, outer, -1)
    turn = jnp.transpose(jnp.broadcast_to(key, (8, MAXB)))[:, 0:1]
    ones = jnp.ones((MAXB, MAXB), I32)
    earlier = lax.broadcasted_iota(I32, (MAXB, MAXB), 0) < lax.broadcasted_iota(I32, (MAXB, MAXB), 1)
    within = jnp.sum(jnp.where((turn == key) & earlier, ones, 0), axis=0, keepdims=True)
    lanes = lax.broadcasted_iota(I32, (MAXB, EDGE), 1)
    held = jnp.sum(jnp.where(turn == lanes, 1, 0), axis=0, keepdims=True)
    pairs = (held + 1) >> 1
    pairs_turn = jnp.transpose(jnp.broadcast_to(pairs, (8, EDGE)))[:, 0:1]
    rows = lax.broadcasted_iota(I32, (EDGE, EDGE), 0)
    upto = jnp.sum(jnp.where(rows <= lax.broadcasted_iota(I32, (EDGE, EDGE), 1), pairs_turn, 0), axis=0, keepdims=True)
    under = lax.broadcasted_iota(I32, (EDGE, MAXB), 0) < key
    start = jnp.sum(jnp.where(under, pairs_turn, 0), axis=0, keepdims=True)
    place = jnp.where(key >= 0, 2 * start + within, -1)
    packed = (ids + 1) + 512 * inner + jnp.where(within == 0, 65536, 0)
    place_turn = jnp.transpose(jnp.broadcast_to(place, (8, MAXB)))[:, 0:1]
    packed_turn = jnp.transpose(jnp.broadcast_to(packed, (8, MAXB)))[:, 0:1]
    taken = place_turn == lax.broadcasted_iota(I32, (MAXB, SLOTS), 1)
    picked = jnp.sum(jnp.where(taken, packed_turn, 0), axis=0, keepdims=True)
    block = picked & 511
    table[0:1, :] = jnp.where(block > 0, block - 1, MAXB)
    table[1:2, :] = (picked >> 9) & 63
    table[2:3, :] = 1 - (picked >> 16)
    table[3:4, :] = jnp.broadcast_to(jnp.concatenate([jnp.maximum(upto - 1, 0)] * 4, axis=1), (1, SLOTS))
    table[4:5, :] = jnp.concatenate([jnp.minimum(held, 1)] * 4, axis=1)
    table[5:8, :] = jnp.zeros((3, SLOTS), I32)


def layer_kernel(
    count, rows, cols, feat_hbm, weight_hbm, bias, blocks_hbm, gout_hbm,
    hidden_hbm, gfeat_hbm, gweight_hbm, gbias_hbm,
    weight, gout, hidden, gfeat, gweight, gbias,
    fwd, bwd, fwd_made, bwd_made,
    blocks, x0, x1, segs, segs2, sib_out, sib_in, z_out, z_in, ax, gp, gt0, gt1, gt2, gt3,
    f_out, f_in, c_out, c_in, own, r_out, r_in,
    ar_mine, ar_cols, ar_x, ar_y, ar_all,
    blocks_sem, feat_sem, table_sem, other_sem, out_sem, x_send, x_recv, sib_send, sib_recv, z_send, z_recv, g_send, g_recv,
    c_send, c_recv, r_send, r_recv, ar_send, ar_recv,
):
    row = lax.axis_index("row")
    col = lax.axis_index("col")
    x, y = row // 4, row % 4
    z, core = col // 2, col % 2
    xs = (x0, x1)
    gts = (gt0, gt1, gt2, gt3)

    def at_x(d):
        return (lax.rem(x + d + 4, 4) * 4 + y, col)

    def at_y(d):
        return (x * 4 + lax.rem(y + d + 4, 4), col)

    def at_z(d):
        return (row, lax.rem(z + d + 4, 4) * 2 + core)

    sibling = (row, z * 2 + 1 - core)

    def remote(src, dst, send, recv, to):
        return pltpu.make_async_remote_copy(
            src_ref=src, dst_ref=dst, send_sem=send, recv_sem=recv, device_id=to, device_id_type=MESH
        )

    load = pltpu.make_async_copy(blocks_hbm.at[0, 0], blocks.at[pl.ds(0, MAXB)], blocks_sem)
    base = (x * 4 + y) * 4
    feats = [
        pltpu.make_async_copy(
            feat_hbm.at[:, :, pl.ds(h * WIDE, WIDE)], xs[h].at[pl.ds(base, 4)], feat_sem.at[h]
        )
        for h in range(HALVES)
    ]
    for copy in feats:
        copy.start()
    others = [
        pltpu.make_async_copy(weight_hbm, weight, other_sem.at[0]),
        pltpu.make_async_copy(gout_hbm, gout, other_sem.at[1]),
    ]
    for copy in others:
        copy.start()
    load.start()
    results = [
        pltpu.make_async_copy(ref, hbm, out_sem.at[i])
        for i, (ref, hbm) in enumerate(
            ((hidden, hidden_hbm), (gfeat, gfeat_hbm), (gweight, gweight_hbm), (gbias, gbias_hbm))
        )
    ]
    barrier = pltpu.get_barrier_semaphore()
    for d in range(1, 4):
        for to in (at_x(d), at_y(d)):
            pl.semaphore_signal(barrier, inc=1, device_id=to, device_id_type=MESH)
    for d in range(1, 8):
        to = (row, lax.rem(col + d, 8))
        pl.semaphore_signal(barrier, inc=1, device_id=to, device_id_type=MESH)

    pl.semaphore_wait(barrier, 13)

    def slab(h, half, e, d):
        first = lax.rem((x if half == 0 else y) - e + 4, 4)
        second = lax.rem((y if half == 0 else x) - d + 4, 4)
        return (first, second) if half == 0 else (second, first)

    def x_copy(h, half, e, d, q, n, sem, to):
        i, j = slab(h, half, e, d)
        part = xs[h].at[pl.ds((i * 4 + j) * 4 + q, n)]
        return remote(part, part, x_send.at[h, half, sem], x_recv.at[h, half, sem], to)

    firsts = (at_x, at_y)
    seconds = (at_y, at_x)

    def x_along(h, half, d):
        return x_copy(h, half, 0, 0, 2 * half, 2, d - 1, firsts[half](d))

    def x_across(h, half, e, way):
        return x_copy(h, half, e, 0, 2 * half, 2, 3 + e * 4 + way, seconds[half](1 - 2 * way))

    def x_pass(h, half, e, way):
        return x_copy(
            h, half, e, 1 - 2 * way, 2 * half + way, 1, 5 + e * 4 + way, seconds[half](1 - 2 * way)
        )

    def x_start(h):
        for half in range(2):
            for d in (1, 3, 2):
                x_along(h, half, d).start()
            for way in range(2):
                x_across(h, half, 0, way).start()

    def x_step(h, e):
        for half in range(2):
            x_along(h, half, e).wait_recv()
            for way in range(2):
                x_across(h, half, e, way).start()

    def x_forward(h, e):
        for half in range(2):
            for way in range(2):
                x_across(h, half, e, way).wait_recv()
                x_pass(h, half, e, way).start()

    def x_finish(h):
        for e in range(4):
            for half in range(2):
                for way in range(2):
                    x_pass(h, half, e, way).wait_recv()

    def x_drain(h):
        for half in range(2):
            for d in (1, 2, 3):
                x_along(h, half, d).wait_send()
            for e in range(4):
                for way in range(2):
                    x_across(h, half, e, way).wait_send()
                    x_pass(h, half, e, way).wait_send()

    def products(table, steps, unroll, wide, one, out, between):
        trips = steps // unroll
        cuts = [trips * i // len(between) for i in range(len(between) + 1)]

        def trip(i, acc):
            for u in range(unroll):
                k = i * unroll + u
                keep = table[2, 2 * k].astype(F32)
                acc = acc * keep + one(table[0, 2 * k], table[0, 2 * k + 1], table[1, 2 * k], table[1, 2 * k + 1])
                out[k] = acc.astype(BF16)
            return acc

        acc = jnp.zeros((wide, EDGE), F32)
        for i, act in enumerate(between):
            act()
            acc = lax.fori_loop(cuts[i], cuts[i + 1], trip, acc)

    def forward(h, between):
        def one(b0, b1, c0, c1):
            pair = jnp.concatenate([blocks[b0], blocks[b1]], axis=1)
            taken = jnp.concatenate([xs[h][c0], xs[h][c1]], axis=0)
            return dot(pair, taken)

        products(fwd, FWD_STEPS, FWD_UNROLL, EDGE, one, segs, between)

    def backward(h, between):
        def one(b0, b1, r0, r1):
            pair = jnp.concatenate([blocks[b0], blocks[b1]], axis=0)
            taken = jnp.concatenate([gts[h][r0], gts[h][r1]], axis=1)
            return dot(taken, pair)

        products(bwd, BWD_STEPS, BWD_UNROLL, THIN, one, segs2, between)

    def segment(table, out, r):
        return out[table[3, r]] * table[4, r].astype(F32).astype(BF16)

    def sib_copy(h, d):
        return remote(sib_out.at[h, d], sib_in.at[h, d], sib_send.at[h, d], sib_recv.at[h, d], sibling)

    def z_copy(h, d):
        return remote(z_out.at[h, d], z_in.at[h, d], z_send.at[h, d], z_recv.at[h, d], at_z(d))

    def sum_start(h):
        for d in (1, 3, 2, 0):
            zz = lax.rem(z + d, 4)
            for q in range(4):
                sib_out[h, d, q] = segment(fwd, segs, (zz * 2 + 1 - core) * 4 + q)
            sib_copy(h, d).start()
        for d in (1, 3, 2, 0):
            zz = lax.rem(z + d, 4)
            for q in range(4):
                z_out[h, d, q] = segment(fwd, segs, (zz * 2 + core) * 4 + q)

    def sum_step(h):
        for d in (1, 3, 2):
            sib_copy(h, d).wait_recv()
            for q in range(4):
                z_out[h, d, q] = (z_out[h, d, q].astype(F32) + sib_in[h, d, q].astype(F32)).astype(BF16)
            z_copy(h, d).start()
        sib_copy(h, 0).wait_recv()

    def sum_finish(h):
        for d in (1, 3, 2):
            z_copy(h, d).wait_recv()
        for q in range(4):
            total = z_out[h, 0, q].astype(F32) + sib_in[h, 0, q].astype(F32)
            for d in (1, 3, 2):
                total = total + z_in[h, d, q].astype(F32)
            ax[q * EDGE:(q + 1) * EDGE, h * WIDE:(h + 1) * WIDE] = total

    def g_part(h, d, k):
        return gts[h].at[pl.ds((lax.rem(z + d + 4, 4) * 2 + k) * 4, 4)]

    def g_across(h, d):
        part = g_part(h, 0, core)
        return remote(part, part, g_send.at[h, d - 1], g_recv.at[h, d - 1], at_z(d))

    def g_sibling(h, d):
        part = g_part(h, -d, core)
        return remote(part, part, g_send.at[h, 3 + d], g_recv.at[h, 3 + d], sibling)

    def g_start(h):
        for d in (1, 3, 2):
            g_across(h, d).start()
        g_sibling(h, 0).start()

    def g_step(h):
        for d in (1, 3, 2):
            g_across(h, d).wait_recv()
            g_sibling(h, d).start()
        for d in (0, 1, 3, 2):
            g_sibling(h, d).wait_recv()

    def f_copy(h, half, way):
        return remote(
            f_out.at[h, half, way], f_in.at[h, half, way],
            c_send.at[h, half, way], c_recv.at[h, half, way], firsts[half](1 - 2 * way),
        )

    def c_copy(h, half, way, q):
        return remote(
            c_out.at[h, half, way, q], c_in.at[h, half, way, q],
            c_send.at[h, half, 2 + 2 * way + q], c_recv.at[h, half, 2 + 2 * way + q], firsts[half](1 - 2 * way),
        )

    def r_copy(h, half, d):
        return remote(
            r_out.at[h, half, d], r_in.at[h, half, d], r_send.at[h, half, d], r_recv.at[h, half, d], seconds[half](d)
        )

    def back_gather(half, d, q, to):
        for s in range(4):
            first = lax.rem((x if half == 0 else y) + d + 4, 4)
            second = lax.rem((y if half == 0 else x) + s, 4)
            i, j = (first, second) if half == 0 else (second, first)
            to[s] = segment(bwd, segs2, (i * 4 + j) * 4 + 2 * half + q)

    def back_start(h):
        for half in range(2):
            for way in range(2):
                back_gather(half, 2, way, f_out.at[h, half, way])
                f_copy(h, half, way).start()
        for half in range(2):
            for way in range(2):
                back_gather(half, 1 - 2 * way, 1 - way, c_out.at[h, half, way, 1 - way])
                c_copy(h, half, way, 1 - way).start()
        for half in range(2):
            for way in range(2):
                back_gather(half, 1 - 2 * way, way, c_out.at[h, half, way, way])
        for half in range(2):
            for q in range(2):
                back_gather(half, 0, q, own.at[h, half, q])

    def back_pass(h):
        for half in range(2):
            for way in range(2):
                f_copy(h, half, way).wait_recv()
                for s in range(4):
                    c_out[h, half, way, way, s] = (
                        c_out[h, half, way, way, s].astype(F32) + f_in[h, half, way, s].astype(F32)
                    ).astype(BF16)
                c_copy(h, half, way, way).start()

    def back_step(h):
        for half in range(2):
            for way in range(2):
                for q in range(2):
                    c_copy(h, half, way, q).wait_recv()
            for s in (2, 1, 3, 0):
                for q in range(2):
                    total = own[h, half, q, s].astype(F32)
                    total = total + c_in[h, half, 0, q, s].astype(F32) + c_in[h, half, 1, q, s].astype(F32)
                    r_out[h, half, s, q] = total.astype(BF16)
                if s:
                    r_copy(h, half, s).start()

    def back_finish(h):
        for half in range(2):
            for d in (1, 3, 2):
                r_copy(h, half, d).wait_recv()
            for q in range(2):
                total = r_out[h, half, 0, q].astype(F32)
                for d in (1, 3, 2):
                    total = total + r_in[h, half, d, q].astype(F32)
                b = 2 * half + q
                gfeat[b * EDGE:(b + 1) * EDGE, h * THIN:(h + 1) * THIN] = jnp.transpose(total).astype(BF16)

    def ar_scatter(d):
        to = lax.rem(col + d, 8)
        return remote(ar_mine.at[to], ar_cols.at[col], ar_send.at[d], ar_recv.at[d], (row, to))

    def ar_over_x(d):
        return remote(ar_x.at[x], ar_x.at[x], ar_send.at[7 + d], ar_recv.at[7 + d], at_x(d))

    def ar_over_y(d):
        return remote(ar_y.at[y], ar_y.at[y], ar_send.at[10 + d], ar_recv.at[10 + d], at_y(d))

    def ar_gather(d):
        to = lax.rem(col + d, 8)
        return remote(ar_all.at[col], ar_all.at[col], ar_send.at[13 + d], ar_recv.at[13 + d], (row, to))

    def ar_start():
        for d in range(1, 8):
            ar_scatter(d).start()
        ar_cols[col] = ar_mine[col]

    def ar_step1():
        for d in range(1, 8):
            ar_scatter(d).wait_recv()
        total = ar_cols[0]
        for i in range(1, 8):
            total = total + ar_cols[i]
        ar_x[x] = total
        for d in range(1, 4):
            ar_over_x(d).start()

    def ar_step2():
        for d in range(1, 4):
            ar_over_x(d).wait_recv()
        ar_y[y] = (ar_x[0] + ar_x[1]) + (ar_x[2] + ar_x[3])
        for d in range(1, 4):
            ar_over_y(d).start()

    def ar_step3():
        for d in range(1, 4):
            ar_over_y(d).wait_recv()
        ar_all[col] = (ar_y[0] + ar_y[1]) + (ar_y[2] + ar_y[3])
        for d in range(1, 8):
            ar_gather(d).start()

    def ar_finish():
        for d in range(1, 8):
            ar_gather(d).wait_recv()
        for i in range(8):
            gweight[i * 32:(i + 1) * 32, :] = ar_all[i, 0:32, :]
        gbias[...] = ar_all[0, 32:33, :]

    def nothing():
        pass

    feats[0].wait()
    x_start(0)
    feats[1].wait()
    x_start(1)
    blocks[MAXB] = jnp.zeros((EDGE, EDGE), BF16)
    one_table(rows[0], cols[0], count[0:1, 0:1], fwd_made)
    put_fwd = pltpu.make_async_copy(fwd_made, fwd, table_sem.at[0])
    put_fwd.start()
    for e in (1, 3, 2):
        x_step(0, e)
    one_table(cols[0], rows[0], count[0:1, 0:1], bwd_made)
    put_bwd = pltpu.make_async_copy(bwd_made, bwd, table_sem.at[1])
    put_bwd.start()
    for e in (0, 1, 3, 2):
        x_forward(0, e)
    for e in (1, 3, 2):
        x_step(1, e)
    x_finish(0)
    put_fwd.wait()
    put_bwd.wait()
    load.wait()
    for copy in others:
        copy.wait()
    forward(0, [functools.partial(x_forward, 1, e) for e in (0, 1, 3, 2)] + [nothing])
    sum_start(0)
    sum_step(0)
    x_finish(1)
    forward(1, [nothing])
    sum_start(1)
    sum_finish(0)
    sum_step(1)
    sum_finish(1)

    bias_sum = jnp.zeros((1, HALVES * WIDE), F32)
    for q in range(4):
        at = slice(q * EDGE, (q + 1) * EDGE)
        total = ax[at, :]
        high = total.astype(BF16)
        low = (total - high.astype(F32)).astype(BF16)
        value = dot(high, weight[...]) + dot(low, weight[...]) + bias[...]
        sig = 1.0 / (1.0 + jnp.exp(-value))
        grad = (gout[at, :].astype(F32) * (sig * (1.0 + value * (1.0 - sig)))).astype(BF16)
        hidden[at, :] = (value * sig).astype(BF16)
        gp[at, :] = grad
        bias_sum = bias_sum + jnp.sum(grad.astype(F32), axis=0, keepdims=True)
        turned = dot_nt(weight[...], grad).astype(BF16)
        for h in range(CHUNKS):
            gts[h][col * 4 + q] = turned[h * THIN:(h + 1) * THIN, :]
    for h in range(CHUNKS):
        g_start(h)
    total = ax[...]
    high = total.astype(BF16)
    low = (total - high.astype(F32)).astype(BF16)
    weight_term = dot_tn(high, gp[...]) + dot_tn(low, gp[...])
    for i in range(8):
        ar_mine[i, 0:32, :] = weight_term[i * 32:(i + 1) * 32, :]
        ar_mine[i, 32:PART, :] = jnp.broadcast_to(bias_sum, (PART - 32, HALVES * WIDE))
    results[0].start()
    g_step(0)
    backward(0, [nothing])
    back_start(0)
    ar_start()
    g_step(1)
    backward(1, [nothing])
    back_pass(0)
    back_start(1)
    ar_step1()
    g_step(2)
    backward(2, [nothing])
    back_pass(1)
    back_step(0)
    back_start(2)
    ar_step2()
    g_step(3)
    backward(3, [nothing])
    back_pass(2)
    back_step(1)
    back_start(3)
    ar_step3()
    back_finish(0)
    back_pass(3)
    back_step(2)
    back_finish(1)
    ar_finish()
    results[2].start()
    results[3].start()
    back_step(3)
    back_finish(2)
    back_finish(3)
    results[1].start()

    for h in range(HALVES):
        x_drain(h)
        for d in range(4):
            sib_copy(h, d).wait_send()
        for d in range(1, 4):
            z_copy(h, d).wait_send()
    for h in range(CHUNKS):
        for d in range(4):
            g_sibling(h, d).wait_send()
        for d in range(1, 4):
            g_across(h, d).wait_send()
            for half in range(2):
                r_copy(h, half, d).wait_send()
        for half in range(2):
            for way in range(2):
                f_copy(h, half, way).wait_send()
                for q in range(2):
                    c_copy(h, half, way, q).wait_send()
    for d in range(1, 4):
        ar_over_x(d).wait_send()
        ar_over_y(d).wait_send()
    for d in range(1, 8):
        ar_scatter(d).wait_send()
        ar_gather(d).wait_send()
    for copy in results:
        copy.wait()


def hand_on_kernel(*refs):
    n = len(refs) // 3
    given, out, held, sems = refs[:n], refs[n:2 * n], refs[2 * n:3 * n], refs[3 * n]
    reads = [pltpu.make_async_copy(given[i], held[i], sems.at[0, i]) for i in range(n)]
    writes = [pltpu.make_async_copy(held[i], out[i], sems.at[1, i]) for i in range(n)]
    for copy in reads:
        copy.start()
    for i in range(n):
        reads[i].wait()
        writes[i].start()
    for copy in writes:
        copy.wait()


def hand_on(*arrays):
    hbm = pl.BlockSpec(memory_space=pltpu.HBM)
    return pl.pallas_call(
        hand_on_kernel,
        out_shape=tuple(jax.ShapeDtypeStruct(a.shape, a.dtype) for a in arrays),
        in_specs=[hbm] * len(arrays),
        out_specs=(hbm,) * len(arrays),
        scratch_shapes=[VMEM(a.shape, a.dtype) for a in arrays] + [pltpu.SemaphoreType.DMA((2, len(arrays)))],
    )(*arrays)


def body(features, weight, bias, adj_blocks, block_rows, block_cols, block_counts, grad_out):
    nodes, hid = features.shape
    sem = pltpu.SemaphoreType.DMA
    block, thin = (EDGE, EDGE), (THIN, EDGE)
    vmem = pl.BlockSpec(memory_space=VMEM)
    hbm = pl.BlockSpec(memory_space=pltpu.HBM)
    hidden, grad_features, grad_weight, grad_bias = pl.pallas_call(
        layer_kernel,
        out_shape=(
            jax.ShapeDtypeStruct((nodes, hid), BF16),
            jax.ShapeDtypeStruct((nodes, hid), BF16),
            jax.ShapeDtypeStruct((hid, hid), F32),
            jax.ShapeDtypeStruct((1, hid), F32),
        ),
        in_specs=[vmem, vmem, vmem, hbm, hbm, vmem, hbm, hbm],
        out_specs=(hbm,) * 4,
        scratch_shapes=[
            VMEM((hid, hid), BF16),
            VMEM((nodes, hid), BF16),
            VMEM((nodes, hid), BF16),
            VMEM((nodes, hid), BF16),
            VMEM((hid, hid), F32),
            VMEM((1, hid), F32),
            SMEM((8, SLOTS), I32),
            SMEM((8, SLOTS), I32),
            VMEM((8, SLOTS), I32),
            VMEM((8, SLOTS), I32),
            VMEM((MAXB + 8, EDGE, EDGE), BF16),
            VMEM((COL_BLOCKS,) + block, BF16),
            VMEM((COL_BLOCKS,) + block, BF16),
            VMEM((FWD_STEPS,) + block, BF16),
            VMEM((BWD_STEPS,) + thin, BF16),
            VMEM((HALVES, 4, 4) + block, BF16),
            VMEM((HALVES, 4, 4) + block, BF16),
            VMEM((HALVES, 4, 4) + block, BF16),
            VMEM((HALVES, 4, 4) + block, BF16),
            VMEM((nodes, hid), F32),
            VMEM((nodes, hid), BF16),
            VMEM((ROW_BLOCKS,) + thin, BF16),
            VMEM((ROW_BLOCKS,) + thin, BF16),
            VMEM((ROW_BLOCKS,) + thin, BF16),
            VMEM((ROW_BLOCKS,) + thin, BF16),
            VMEM((CHUNKS, 2, 2, 4) + thin, BF16),
            VMEM((CHUNKS, 2, 2, 4) + thin, BF16),
            VMEM((CHUNKS, 2, 2, 2, 4) + thin, BF16),
            VMEM((CHUNKS, 2, 2, 2, 4) + thin, BF16),
            VMEM((CHUNKS, 2, 2, 4) + thin, BF16),
            VMEM((CHUNKS, 2, 4, 2) + thin, BF16),
            VMEM((CHUNKS, 2, 4, 2) + thin, BF16),
            VMEM((8, PART, hid), F32),
            VMEM((8, PART, hid), F32),
            VMEM((4, PART, hid), F32),
            VMEM((4, PART, hid), F32),
            VMEM((8, PART, hid), F32),
            sem, sem((HALVES,)), sem((2,)), sem((2,)), sem((4,)),
            sem((HALVES, 2, 19)), sem((HALVES, 2, 19)),
            sem((HALVES, 4)), sem((HALVES, 4)),
            sem((HALVES, 4)), sem((HALVES, 4)),
            sem((CHUNKS, 7)), sem((CHUNKS, 7)),
            sem((CHUNKS, 2, 6)), sem((CHUNKS, 2, 6)),
            sem((CHUNKS, 2, 4)), sem((CHUNKS, 2, 4)),
            sem((21,)), sem((21,)),
        ],
        compiler_params=pltpu.CompilerParams(
            collective_id=0, has_side_effects=True, vmem_limit_bytes=56 * 2**20
        ),
        cost_estimate=pl.CostEstimate(flops=8 * 10**9, bytes_accessed=16 * 2**20, transcendentals=2**18),
    )(
        block_counts, block_rows, block_cols, features.reshape(nodes // EDGE, EDGE, hid), weight,
        bias.reshape(1, hid), adj_blocks, grad_out,
    )
    hidden, grad_features, grad_weight, grad_bias = hand_on(hidden, grad_features, grad_weight, grad_bias)
    return hidden, grad_features, grad_weight, grad_bias.reshape(hid)


def solution(mesh):
    in_specs = (
        P(("row", "col"), None),
        P(),
        P(),
        P("row", "col", None, None, None),
        P("row", "col", None),
        P("row", "col", None),
        P("row", "col"),
        P(("row", "col"), None),
    )
    out_specs = (P(("row", "col"), None), P(("row", "col"), None), P(), P())
    return jax.shard_map(body, mesh=mesh, in_specs=in_specs, out_specs=out_specs, check_vma=False)
```

time: 133 us -> 103 us (0.77)
  Pallas kernels: 125 us -> 101 us
  local copies, waits for them, and re-layouts: 6.22 us -> 0 us
    pallas_call x1, Pallas kernels: 123 us -> 99.5 us  [body(): pl.pallas_call(layer_kernel, out_shape=(jax.ShapeDtypeStruct((nodes, hid)...]
    unnamed x4 -> x0, local copies, waits for them, and re-layouts: 6.22 us -> none
where the time goes in v2:
time: 103 us
  Pallas kernels  101 us (98%)
  between operations  1.29 us (1%)
    pallas_call x1, Pallas kernels, body(): pl.pallas_call(layer_kernel, out_shape=(jax.ShapeDtypeStruct((nodes, hid)...  99.5 us

profile of v2, /device:TPU:0, one launch (start us, length us, event | category | flops | bytes accessed | tf_op | source)
XLA Modules:
  0.0 102.7 jit_solution(15687615373142014205)
XLA Ops:
  1.3 99.5 %shard_map.111 = (bf16[512,256]{1,0:T(8,128)(2,1)}, bf16[512,256]{1,0:T(8,128)(2,1)}, f32[256,256]{1,0:T(8,128)}, f32[1,256]{1,0:T(1,128)}) custom-call(s32[1,1]{1,0:T(1,128)S(6)} %copy.12.count, s32[1,1,384]{2,1,0:T(1,128)} %rows.1, s32[1,1,384]{2,1,0:T(1,128)} %cols.1, bf16[4,128,256]{2,1,0:T(8,128)(2,1)} %bitcast.3, bf16[256,256]{1,0:T(8,128)(2,1)} %weight_hbm.1, ...), custom_call_target="tpu_custom_call" | custom-call | flops 8000000000 | bytes 16777216 | tf_op jit(solution)/shard_map/pallas_call | solution.py:569
  100.8 1.9 %shard_map.112 = (bf16[512,256]{1,0:T(8,128)(2,1)}, bf16[512,256]{1,0:T(8,128)(2,1)}, f32[256,256]{1,0:T(8,128)}, f32[1,256]{1,0:T(1,128)}) custom-call(bf16[512,256]{1,0:T(8,128)(2,1)} %get-tuple-element.12.refs_0_, bf16[512,256]{1,0:T(8,128)(2,1)} %get-tuple-element.13.refs_1_, f32[256,256]{1,0:T(8,128)} %get-tuple-element.14.refs_2_, ...), custom_call_target="tpu_custom_call" | custom-call | tf_op jit(solution)/shard_map/pallas_call | solution.py:554

commit v3 on v2

--- a/solution.py
+++ b/solution.py
@@ -162,16 +162,29 @@
             h, half, e, 1 - 2 * way, 2 * half + way, 1, 5 + e * 4 + way, seconds[half](1 - 2 * way)
         )
 
+    def x_relay(h, half, way):
+        return x_copy(
+            h, half, 1 - 2 * way, 0, 2 * half + way, 1, 1 + 18 * way, firsts[half](1 - 2 * way)
+        )
+
     def x_start(h):
         for half in range(2):
-            for d in (1, 3, 2):
+            for d in (1, 3):
                 x_along(h, half, d).start()
             for way in range(2):
                 x_across(h, half, 0, way).start()
 
+    def x_relay_start(h):
+        for half in range(2):
+            for way in range(2):
+                x_along(h, half, 1 + 2 * way).wait_recv()
+                x_relay(h, half, way).start()
+
     def x_step(h, e):
         for half in range(2):
-            x_along(h, half, e).wait_recv()
+            if e == 2:
+                for way in range(2):
+                    x_relay(h, half, way).wait_recv()
             for way in range(2):
                 x_across(h, half, e, way).start()
 
@@ -189,8 +202,10 @@
 
     def x_drain(h):
         for half in range(2):
-            for d in (1, 2, 3):
+            for d in (1, 3):
                 x_along(h, half, d).wait_send()
+            for way in range(2):
+                x_relay(h, half, way).wait_send()
             for e in range(4):
                 for way in range(2):
                     x_across(h, half, e, way).wait_send()
@@ -239,7 +254,7 @@
         return remote(z_out.at[h, d], z_in.at[h, d], z_send.at[h, d], z_recv.at[h, d], at_z(d))
 
     def sum_start(h):
-        for d in (1, 3, 2, 0):
+        for d in (2, 1, 3, 0):
             zz = lax.rem(z + d, 4)
             for q in range(4):
                 sib_out[h, d, q] = segment(fwd, segs, (zz * 2 + 1 - core) * 4 + q)
@@ -250,7 +265,7 @@
                 z_out[h, d, q] = segment(fwd, segs, (zz * 2 + core) * 4 + q)
 
     def sum_step(h):
-        for d in (1, 3, 2):
+        for d in (2, 1, 3):
             sib_copy(h, d).wait_recv()
             for q in range(4):
                 z_out[h, d, q] = (z_out[h, d, q].astype(F32) + sib_in[h, d, q].astype(F32)).astype(BF16)
@@ -278,7 +293,7 @@
         return remote(part, part, g_send.at[h, 3 + d], g_recv.at[h, 3 + d], sibling)
 
     def g_start(h):
-        for d in (1, 3, 2):
+        for d in (2, 1, 3):
             g_across(h, d).start()
         g_sibling(h, 0).start()
 
@@ -424,8 +439,11 @@
     one_table(rows[0], cols[0], count[0:1, 0:1], fwd_made)
     put_fwd = pltpu.make_async_copy(fwd_made, fwd, table_sem.at[0])
     put_fwd.start()
-    for e in (1, 3, 2):
+    x_relay_start(0)
+    for e in (1, 3):
         x_step(0, e)
+    x_relay_start(1)
+    x_step(0, 2)
     one_table(cols[0], rows[0], count[0:1, 0:1], bwd_made)
     put_bwd = pltpu.make_async_copy(bwd_made, bwd, table_sem.at[1])
     put_bwd.start()
@@ -445,8 +463,8 @@
     x_finish(1)
     forward(1, [nothing])
     sum_start(1)
+    sum_step(1)
     sum_finish(0)
-    sum_step(1)
     sum_finish(1)
 
     bias_sum = jnp.zeros((1, HALVES * WIDE), F32)
@@ -615,7 +633,7 @@
             VMEM((4, PART, hid), F32),
             VMEM((8, PART, hid), F32),
             sem, sem((HALVES,)), sem((2,)), sem((2,)), sem((4,)),
-            sem((HALVES, 2, 19)), sem((HALVES, 2, 19)),
+            sem((HALVES, 2, 20)), sem((HALVES, 2, 20)),
             sem((HALVES, 4)), sem((HALVES, 4)),
             sem((HALVES, 4)), sem((HALVES, 4)),
             sem((CHUNKS, 7)), sem((CHUNKS, 7)),

time: 103 us -> 99.4 us (0.965)
  Pallas kernels: 101 us -> 97.9 us
    pallas_call x1, Pallas kernels: 99.5 us -> 96 us  [body(): pl.pallas_call(layer_kernel, out_shape=(jax.ShapeDtypeStruct((nodes, hid)...]
where the time goes in v3:
time: 99.4 us; the launch traced here: 99.2 us
  Pallas kernels  97.9 us (98%)
  between operations  1.29 us (1%)
    pallas_call x1, Pallas kernels, body(): pl.pallas_call(layer_kernel, out_shape=(jax.ShapeDtypeStruct((nodes, hid)...  96 us

profile of v3, /device:TPU:0, one launch (start us, length us, event | category | flops | bytes accessed | tf_op | source)
XLA Modules:
  0.0 99.2 jit_solution(7656858363361493469)
XLA Ops:
  1.3 96.0 %shard_map.111 = (bf16[512,256]{1,0:T(8,128)(2,1)}, bf16[512,256]{1,0:T(8,128)(2,1)}, f32[256,256]{1,0:T(8,128)}, f32[1,256]{1,0:T(1,128)}) custom-call(s32[1,1]{1,0:T(1,128)S(6)} %copy.12.count, s32[1,1,384]{2,1,0:T(1,128)} %rows.1, s32[1,1,384]{2,1,0:T(1,128)} %cols.1, bf16[4,128,256]{2,1,0:T(8,128)(2,1)} %bitcast.3, bf16[256,256]{1,0:T(8,128)(2,1)} %weight_hbm.1, ...), custom_call_target="tpu_custom_call" | custom-call | flops 8000000000 | bytes 16777216 | tf_op jit(solution)/shard_map/pallas_call | solution.py:587
  97.3 1.9 %shard_map.112 = (bf16[512,256]{1,0:T(8,128)(2,1)}, bf16[512,256]{1,0:T(8,128)(2,1)}, f32[256,256]{1,0:T(8,128)}, f32[1,256]{1,0:T(1,128)}) custom-call(bf16[512,256]{1,0:T(8,128)(2,1)} %get-tuple-element.12.refs_0_, bf16[512,256]{1,0:T(8,128)(2,1)} %get-tuple-element.13.refs_1_, f32[256,256]{1,0:T(8,128)} %get-tuple-element.14.refs_2_, ...), custom_call_target="tpu_custom_call" | custom-call | tf_op jit(solution)/shard_map/pallas_call | solution.py:572

commit v4 on v3

--- a/solution.py
+++ b/solution.py
@@ -459,9 +459,8 @@
         copy.wait()
     forward(0, [functools.partial(x_forward, 1, e) for e in (0, 1, 3, 2)] + [nothing])
     sum_start(0)
-    sum_step(0)
     x_finish(1)
-    forward(1, [nothing])
+    forward(1, [functools.partial(sum_step, 0), nothing])
     sum_start(1)
     sum_step(1)
     sum_finish(0)

time: 99.4 us -> 99.6 us (level)
  no operation moved by 1% of the time
where the time goes in v4:
time: 99.6 us; the launch traced here: 99.4 us
  Pallas kernels  98.1 us (98%)
  between operations  1.29 us (1%)
    pallas_call x1, Pallas kernels, body(): pl.pallas_call(layer_kernel, out_shape=(jax.ShapeDtypeStruct((nodes, hid)...  96.2 us

profile of v4, /device:TPU:0, one launch (start us, length us, event | category | flops | bytes accessed | tf_op | source)
XLA Modules:
  0.0 99.4 jit_solution(7300773412211874623)
XLA Ops:
  1.3 96.2 %shard_map.111 = (bf16[512,256]{1,0:T(8,128)(2,1)}, bf16[512,256]{1,0:T(8,128)(2,1)}, f32[256,256]{1,0:T(8,128)}, f32[1,256]{1,0:T(1,128)}) custom-call(s32[1,1]{1,0:T(1,128)S(6)} %copy.12.count, s32[1,1,384]{2,1,0:T(1,128)} %rows.1, s32[1,1,384]{2,1,0:T(1,128)} %cols.1, bf16[4,128,256]{2,1,0:T(8,128)(2,1)} %bitcast.3, bf16[256,256]{1,0:T(8,128)(2,1)} %weight_hbm.1, ...), custom_call_target="tpu_custom_call" | custom-call | flops 8000000000 | bytes 16777216 | tf_op jit(solution)/shard_map/pallas_call | solution.py:586
  97.5 1.9 %shard_map.112 = (bf16[512,256]{1,0:T(8,128)(2,1)}, bf16[512,256]{1,0:T(8,128)(2,1)}, f32[256,256]{1,0:T(8,128)}, f32[1,256]{1,0:T(1,128)}) custom-call(bf16[512,256]{1,0:T(8,128)(2,1)} %get-tuple-element.12.refs_0_, bf16[512,256]{1,0:T(8,128)(2,1)} %get-tuple-element.13.refs_1_, f32[256,256]{1,0:T(8,128)} %get-tuple-element.14.refs_2_, ...), custom_call_target="tpu_custom_call" | custom-call | tf_op jit(solution)/shard_map/pallas_call | solution.py:571
